TPU v7x, 256 devices: a whole 4x4x8 slice. The times are simulated.
256 devices in a mesh: bead: 32 (over z_hi, x, core), dom: 8 (over y, z_lo).
Axes of the slice: x: 4, y: 4, z: 8 (z_hi: 4, z_lo: 2; z = z_hi * 2 + z_lo), core: 2. Of those that a mesh axis runs over, the one named last changes fastest.
Arguments:
- positions: float32 [3, 32, 4096], P(None, 'bead', 'dom'), may hold values from -2.5 to 2.5
- momenta: float32 [3, 32, 4096], P(None, 'bead', 'dom'), may hold values from -6 to 6
- forces: float32 [3, 32, 4096], P(None, 'bead', 'dom'), may hold values from -6 to 6
- masses: float32 [4096], P('dom'), may hold values from 1 to 16
- charges: float32 [4096], P('dom'), may hold values from -1 to 1
- embedding: bfloat16 [4096, 240], P('dom'), may hold values from -6 to 6
- neighbours: int32 [8, 4096], P(None, 'dom'), may hold values from 0 to 895
- send_rows: int32 [3072], P('dom'), may hold values from 0 to 511
- wavevectors: int32 [3, 16384], replicated, may hold values from -12 to 12, as said below
- radial_weight: bfloat16 [2, 16, 240], replicated, may hold values from -1.5 to 1.5
- mix_weight: bfloat16 [2, 240, 240], replicated, may hold values from -0.375 to 0.375
- update_weight: bfloat16 [2, 240, 240], replicated, may hold values from -0.375 to 0.375
- readout_weight: bfloat16 [240, 240], replicated, may hold values from -0.375 to 0.375
- energy_weight: float32 [240], replicated, may hold values from -0.375 to 0.375
Outputs:
- next_positions: float32 [3, 32, 4096], P(None, 'bead', 'dom')
- next_momenta: float32 [3, 32, 4096], P(None, 'bead', 'dom')
- next_forces: float32 [3, 32, 4096], P(None, 'bead', 'dom')
Inputs may be any that keep to these rules, and one draw needn't show every extreme that they name: `wavevectors`: no component is zero.
All inputs are finite; a program needn't handle non-finite values.
Results may differ from a plain program's by a relative error of at most 0.0065.
Values may be sent and summed in bfloat16 or wider, within the bound.
A program may use at most 64 MiB of HBM per device.

v0:
```python
import math
import jax
import jax.numpy as jnp
from jax import lax
from jax.sharding import PartitionSpec as P

step_dt = 0.25
omega_cycle = 1.6
box_length = 4.0
ewald_sigma = 0.002
ewald_gain = 48.0
norm_eps = 1e-06
peak_frequency = lax.Precision.HIGHEST


def extended(cells, sides, width):
    for axis, dim in sides:
        count = lax.axis_size(axis)
        head = lax.slice_in_dim(cells, 0, width, axis=dim)
        tail = lax.slice_in_dim(cells, cells.shape[dim] - width, cells.shape[dim], axis=dim)
        cells = jnp.concatenate(
            [
                lax.ppermute(tail, axis, [(i, (i + 1) % count) for i in range(count)]),
                cells,
                lax.ppermute(head, axis, [((i + 1) % count, i) for i in range(count)]),
            ],
            axis=dim,
        )
    return cells


def mode_matrix(length):
    row_index = jnp.arange(length, dtype=jnp.int32)[:, None]
    column_index = jnp.arange(length, dtype=jnp.int32)[None, :]
    angles = 2.0 * math.pi / length * (row_index * column_index % length).astype(jnp.float32)
    single_norm = math.sqrt(1.0 / length)
    double_norm = math.sqrt(2.0 / length)
    parity = (1 - 2 * (row_index % 2)).astype(jnp.float32)
    middle = length // 2
    normal_transform = jnp.where(
        column_index == 0,
        single_norm,
        jnp.where(
            column_index < middle,
            double_norm * jnp.cos(angles),
            jnp.where(column_index == middle, single_norm * parity, double_norm * jnp.sin(angles)),
        ),
    )
    return normal_transform


def propagate(normal_mode_positions, normal_mode_momentum, masses):
    length = normal_mode_positions.shape[1]
    orders = jnp.arange(length, dtype=jnp.float32)
    omegas = 2.0 * omega_cycle * jnp.sin(math.pi * orders / length)
    cosine = jnp.cos(omegas * step_dt)[:, None]
    sines = jnp.sin(omegas * step_dt)
    omega_safe = jnp.where(orders == 0.0, 1.0, omegas)
    drift = jnp.where(orders == 0.0, step_dt, sines / omega_safe)[:, None]
    spring = (omegas * sines)[:, None]
    next_coords = cosine * normal_mode_positions + drift * normal_mode_momentum / masses
    next_moment = cosine * normal_mode_momentum - spring * masses * normal_mode_positions
    return (next_coords, next_moment)


def ewald_coef(reciprocal, atom_total):
    square = jnp.sum(reciprocal * reciprocal, 0)
    return (
        ewald_gain
        / math.sqrt(reciprocal.shape[1] * atom_total)
        * jnp.exp(-ewald_sigma * square)
        / square
    )


def phase_sums(reciprocal, centre, charge):
    phases = jnp.dot(reciprocal.T, centre, precision=peak_frequency)
    return (
        jnp.dot(jnp.cos(phases), charge, precision=peak_frequency),
        jnp.dot(jnp.sin(phases), charge, precision=peak_frequency),
    )


def ewald_force(reciprocal, centre, charge, cosine_sum, sine_sum, damping):
    phases = jnp.dot(reciprocal.T, centre, precision=peak_frequency)
    weight = (damping * cosine_sum)[:, None] * jnp.sin(phases) - (damping * sine_sum)[
        :, None
    ] * jnp.cos(phases)
    return 2.0 * charge * jnp.dot(reciprocal, weight, precision=peak_frequency)


def long_range(reciprocal, centre, charge, damping):
    cosine_part, sine_part = phase_sums(reciprocal, centre, charge)
    cosine_sum, sine_sum = lax.psum((cosine_part, sine_part), ("bead", "dom"))
    return ewald_force(reciprocal, centre, charge, cosine_sum, sine_sum, damping)


def advance(normal_mode_entries, mass_share, charge_share, reciprocal, damping):
    normal_mode_positions, normal_mode_momentum = propagate(
        normal_mode_entries[:3], normal_mode_entries[3:], mass_share
    )
    centre = normal_mode_positions[:, 0, :] / math.sqrt(normal_mode_entries.shape[1])
    long_force = long_range(reciprocal, centre, charge_share, damping)
    return (jnp.concatenate([normal_mode_positions, normal_mode_momentum], 0), long_force)


def layer_apply(
    hidden_own,
    extended_rows,
    extended_coords,
    neighbour_table,
    radial,
    mixing,
    update,
    radial_rates,
):
    owned_count = hidden_own.shape[0]
    owners = extended_coords[:, :owned_count]
    others = extended_coords[:, neighbour_table]
    offset = others - owners[:, None, :]
    distance = jnp.sum(offset * offset, 0)
    basis = (1.0 / (1.0 + radial_rates[:, None, None] * distance[None])).astype(jnp.bfloat16)
    edge_weight = jnp.einsum("mka,mf->kaf", basis, radial, preferred_element_type=jnp.float32)
    message = jnp.sum(edge_weight * extended_rows[neighbour_table], 0)
    scaled = message * lax.rsqrt(jnp.mean(message * message, -1, keepdims=True) + norm_eps)
    gated = jax.nn.silu(
        jnp.dot(scaled.astype(jnp.bfloat16), mixing, preferred_element_type=jnp.float32)
    ).astype(jnp.bfloat16)
    return hidden_own + jnp.dot(gated, update, preferred_element_type=jnp.float32)


def readout(hidden, readout_weight, energy_weight):
    activation = jax.nn.silu(
        jnp.dot(hidden.astype(jnp.bfloat16), readout_weight, preferred_element_type=jnp.float32)
    )
    return jnp.sum(activation * energy_weight)


def short_forces(
    coords,
    embedding,
    neighbours,
    send_rows,
    radial_weight,
    mix_weight,
    update_weight,
    readout_weight,
    energy_weight,
):
    owned_rows = coords.shape[2]
    ghost_rows = send_rows.shape[0] // 2
    to_before = send_rows[:ghost_rows]
    to_after = send_rows[ghost_rows:]
    radial_rates = 0.125 * 2.0 ** (0.5 * jnp.arange(radial_weight.shape[1], dtype=jnp.float32))
    apply_layer = jax.vmap(layer_apply, in_axes=(0, 0, 0, None, None, None, None, None))
    beside_all = extended(coords[:, :, send_rows], (("dom", 2),), ghost_rows)
    extended_coords = jnp.concatenate(
        [coords, beside_all[:, :, :ghost_rows], beside_all[:, :, 3 * ghost_rows :]], 2
    )
    extended_coords = jnp.moveaxis(extended_coords, 1, 0)
    hidden = embedding.astype(jnp.float32)[None]
    stored = []
    for number in range(mix_weight.shape[0]):
        rounded = hidden.astype(jnp.bfloat16)
        arrived = extended(rounded[:, send_rows, :], (("dom", 1),), ghost_rows)
        extended_rows = jnp.concatenate(
            [rounded, arrived[:, :ghost_rows], arrived[:, 3 * ghost_rows :]], 1
        ).astype(jnp.float32)
        stored.append((hidden, extended_rows))
        hidden = apply_layer(
            hidden,
            extended_rows,
            extended_coords,
            neighbours,
            radial_weight[number],
            mix_weight[number],
            update_weight[number],
            radial_rates,
        )
    cotan = jax.vmap(jax.grad(readout), in_axes=(0, None, None))(
        hidden, readout_weight, energy_weight
    )
    position_grad = jnp.zeros_like(extended_coords)
    for number in reversed(range(mix_weight.shape[0])):
        layer_input, extended_rows = stored[number]

        def local_layer(hidden_part, rows_part, coords_part):
            return apply_layer(
                hidden_part,
                rows_part,
                coords_part,
                neighbours,
                radial_weight[number],
                mix_weight[number],
                update_weight[number],
                radial_rates,
            )

        unused, pullback = jax.vjp(local_layer, layer_input, extended_rows, extended_coords)
        input_grad, feature_grad, position_part = pullback(cotan)
        position_grad = position_grad + position_part
        if number > 0:
            returned = extended(
                feature_grad[:, owned_rows:, :].astype(jnp.bfloat16), (("dom", 1),), ghost_rows
            ).astype(jnp.float32)
            owned_grad = (
                feature_grad[:, :owned_rows, :]
                .at[:, to_before, :]
                .add(returned[:, :ghost_rows])
                .at[:, to_after, :]
                .add(returned[:, 3 * ghost_rows :])
            )
            cotan = input_grad + owned_grad.astype(jnp.bfloat16).astype(jnp.float32)
    returned = extended(position_grad[:, :, owned_rows:], (("dom", 2),), ghost_rows)
    owned_force = (
        position_grad[:, :, :owned_rows]
        .at[:, :, to_before]
        .add(returned[:, :, :ghost_rows])
        .at[:, :, to_after]
        .add(returned[:, :, 3 * ghost_rows :])
    )
    return -jnp.moveaxis(owned_force, 0, 1)


def local(
    positions,
    momenta,
    forces,
    masses,
    charges,
    embedding,
    neighbours,
    send_rows,
    wavevectors,
    radial_weight,
    mix_weight,
    update_weight,
    readout_weight,
    energy_weight,
):
    beads_here = positions.shape[1]
    atom_count = positions.shape[2]
    bead_devices = lax.axis_size("bead")
    bead_slot = lax.axis_index("bead")
    bead_count = beads_here * bead_devices
    atom_share = atom_count // bead_devices
    normal_transform = mode_matrix(bead_count)
    bead_rows = lax.dynamic_slice_in_dim(normal_transform, bead_slot * beads_here, beads_here, 0)
    mass_share = lax.dynamic_slice_in_dim(masses, bead_slot * atom_share, atom_share, 0)
    charge_share = lax.dynamic_slice_in_dim(charges, bead_slot * atom_share, atom_share, 0)
    reciprocal = wavevectors.astype(jnp.float32) * (2.0 * math.pi / box_length)
    damping = ewald_coef(reciprocal, atom_count * lax.axis_size("dom"))
    coords_now, moment_now, force_now = (positions, momenta, forces)
    kicked = moment_now + 0.5 * step_dt * force_now
    stacked_arrays = jnp.concatenate([coords_now, kicked], 0)
    segment = stacked_arrays
    summed = lax.psum_scatter(
        jnp.einsum("bk,cba->ack", bead_rows, segment, precision=peak_frequency),
        "bead",
        scatter_dimension=0,
        tiled=True,
    )
    normal_mode_entries = jnp.transpose(summed, (1, 2, 0))
    joined, long_force = advance(normal_mode_entries, mass_share, charge_share, reciprocal, damping)
    packed = jnp.concatenate(
        [jnp.transpose(joined, (2, 0, 1)).reshape(atom_share, 6 * bead_count), long_force.T], 1
    )
    segment = lax.all_gather(packed, "bead", axis=0, tiled=True)
    row_count = segment.shape[0]
    coords = segment[:, : 6 * bead_count].reshape(row_count, 6, bead_count)
    restored = jnp.einsum("bk,ack->cba", bead_rows, coords, precision=peak_frequency)
    spread = segment[:, 6 * bead_count :].T[:, None, :]
    arrived = jnp.concatenate([restored, spread], 0)
    coords_now = arrived[:3]
    short_force = short_forces(
        coords_now,
        embedding,
        neighbours,
        send_rows,
        radial_weight,
        mix_weight,
        update_weight,
        readout_weight,
        energy_weight,
    )
    force_now = short_force + arrived[6:]
    moment_now = arrived[3:6] + 0.5 * step_dt * force_now
    return (coords_now, moment_now, force_now)


def solution(mesh):
    placed = (
        P(None, "bead", "dom"),
        P(None, "bead", "dom"),
        P(None, "bead", "dom"),
        P("dom"),
        P("dom"),
        P("dom", None),
        P(None, "dom"),
        P("dom"),
        P(),
        P(),
        P(),
        P(),
        P(),
        P(),
    )
    return jax.shard_map(
        local,
        mesh=mesh,
        in_specs=placed,
        out_specs=(P(None, "bead", "dom"), P(None, "bead", "dom"), P(None, "bead", "dom")),
        check_vma=False,
    )
```

profile of v0, /device:TPU:2, one launch (start us, length us, event | category | flops | bytes accessed | tf_op | source)
XLA Modules:
  0.0 636.9 jit_solution(1569555388232173794)
XLA Ops:
  10.3 2.0 multiply_bitcast_fusion
  12.5 2.1 gather_fusion.2
  14.6 4.4 collective-permute-start.3
  21.1 85.0 %reduce-scatter.2.cloned.1.call-done = f32[16,6,32]{2,1,0:T(8,128)} async-done(((f32[512,6,32]{2,1,0:T(8,128)}), f32[16,6,32]{2,1,0:T(8,128)}) %reduce-scatter.2.cloned.1.call-update) | async-done | bytes 12304 | tf_op jit(solution)/shard_map/reduce_scatter | solution.py:257
  107.1 8.0 %fusion.207 = (f32[16384,16]{0,1:T(8,128)S(1)}, f32[16384,16]{0,1:T(8,128)S(1)}) fusion(f32[3,16]{1,0:T(4,128)S(1)} %fusion.160, s32[3,16384]{1,0:T(4,128)S(1)} %copy-done.11), kind=kOutput, calls=%fused_computation.258 | convolution fusion | flops 9535488 | bytes 2293952 | tf_op jit(solution)/shard_map/dot_general | solution.py:77
  115.0 1.3 fusion.186
  116.3 1.3 fusion.188
  117.8 240.3 %all-reduce.5.cloned.1.call-done = (f32[16384]{0:T(1024)}, f32[16384]{0:T(1024)}) async-done(((f32[16384]{0:T(1024)}, f32[16384]{0:T(1024)}), (f32[16384]{0:T(1024)}, f32[16384]{0:T(1024)})) %all-reduce.5.cloned.1.call-update) | async-done | bytes 131088 | tf_op jit(solution)/shard_map/psum | solution.py:94
  359.0 1.4 convolution_multiply_fusion
  360.6 41.0 %all_gather.3 = f32[512,195]{1,0:T(8,128)S(1)} all-gather(f32[16,195]{1,0:T(8,128)S(1)} %pad_maximum_fusion.5), channel_id=1, replica_groups=mesh['bead'=32,'dom'=8] {'bead'}, dimensions={0}, use_global_device_ids=true | all-gather | bytes 411840 | tf_op jit(solution)/shard_map/all_gather | solution.py:268
  403.5 1.9 collective-permute-start.1
  406.1 16.1 %gather_fusion.3 = f32[4096,240]{1,0:T(8,128)} fusion(f32[896,240]{1,0:T(8,128)S(1)} %fusion.95, s32[4096]{0:T(1024)S(1)} %broadcast_clamp_fusion), kind=kCustom, calls=%fused_computation.3 | custom fusion | bytes 7880704 | tf_op jit(solution)/shard_map/vmap()/gather | solution.py:124
  422.2 5.3 copy.144
  427.5 5.3 copy.134
  433.6 10.8 %gather_fusion.1 = f32[4096,3]{1,0:T(8,128)S(1)} fusion(f32[3,896]{0,1:T(8,128)S(1)} %get-tuple-element.32, s32[4096]{0:T(1024)S(1)} %broadcast_clamp_fusion), kind=kCustom, calls=%fused_computation.1 | custom fusion | bytes 114688 | tf_op jit(solution)/shard_map/jvp(vmap())/gather | solution.py:119
  445.1 2.9 multiply_reduce_fusion.1
  449.7 2.1 gather_fusion.4
  452.0 4.0 collective-permute-start.5
  456.2 2.6 fusion.124
  459.8 3.4 collective-permute-done.4
  464.2 1.5 copy.137
  465.7 16.1 %gather_fusion.5 = f32[4096,240]{1,0:T(8,128)} fusion(f32[896,240]{1,0:T(8,128)S(1)} %copy.137, s32[4096]{0:T(1024)S(1)} %broadcast_clamp_fusion), kind=kCustom, calls=%fused_computation.5 | custom fusion | bytes 7880704 | tf_op jit(solution)/shard_map/vmap()/gather | solution.py:124
  481.7 5.3 copy.139
  487.0 4.4 multiply_reduce_fusion
  492.5 2.6 fusion.13
  495.1 2.1 convolution_convert_fusion.4
  497.3 2.5 multiply_reduce_fusion.4
  499.8 1.2 add_add_fusion.1
  501.7 4.7 broadcast_multiply_fusion
  506.4 5.2 copy.154
  511.6 23.1 %scatter_custom_fusion.1 = f32[896,240]{1,0:T(8,128)S(1)} fusion(s32[4096]{0:T(1024)S(1)} %bitcast.302, f32[4096,240]{1,0:T(8,128)} %bitcast.291, f32[]{:T(128)} %constant.51.clone.1), kind=kCustom, calls=%fused_computation.103 | custom fusion | flops 983040 | bytes 860672 | tf_op jit(solution)/shard_map/transpose(jvp(vmap()))/scatter-add | solution.py:124
  536.4 1.2 collective-permute-start.7
  538.4 5.3 copy.140
  543.7 3.1 fusion.59
  548.6 3.9 scatter_custom_fusion.2
  552.5 3.5 scatter_custom_fusion.3
  555.9 1.2 copy.143
  557.1 2.5 multiply_reduce_fusion.3
  560.9 2.8 fusion.38
  563.7 3.1 add_multiply_fusion
  566.8 1.9 reduce_sum.128
  571.7 22.8 %scatter_fusion = f32[3,896]{0,1:T(8,128)S(1)} fusion(f32[3,896]{0,1:T(8,128)S(1)} %pad_bitcast_fusion.1, s32[4096]{0:T(1024)S(1)} %bitcast.303, f32[4096,3]{1,0:T(8,128)} %bitcast.288), kind=kCustom, calls=%fused_computation.6 | custom fusion | flops 12288 | bytes 163840 | tf_op jit(solution)/shard_map/transpose(jvp(vmap()))/scatter-add | solution.py:119
  594.6 21.9 %scatter_fusion.1 = f32[3,896]{0,1:T(8,128)} fusion(f32[3,896]{0,1:T(8,128)} %pad_bitcast_fusion, s32[4096]{0:T(1024)S(1)} %bitcast.304, f32[4096,3]{1,0:T(8,128)S(1)} %bitcast.287), kind=kCustom, calls=%fused_computation.10 | custom fusion | flops 12288 | bytes 163840 | tf_op jit(solution)/shard_map/transpose(jvp(vmap()))/scatter-add | solution.py:119
  617.6 1.5 collective-permute-start.8
  619.1 2.7 collective-permute-start.9
  621.8 2.6 collective-permute-done.8
  624.4 1.8 scatter_custom_fusion.5
  626.2 1.9 scatter_custom_fusion.6
  (150 shorter events, 28.6 us)
Async XLA Ops:
  7.2 485.4 %copy-start = (bf16[240,240]{1,0:T(8,128)(2,1)S(1)}, bf16[240,240]{1,0:T(8,128)(2,1)}, u32[]{:S(2)}) copy-start(bf16[240,240]{1,0:T(8,128)(2,1)} %param.26) | copy-start | bytes 345604
  7.2 5.2 copy-start.14
  7.2 5.3 copy-start.26
  7.2 12.7 %copy-start.21 = (s32[8,512]{1,0:T(8,128)S(1)}, s32[8,512]{1,0:T(8,128)}, u32[]{:S(2)}) copy-start(s32[8,512]{1,0:T(8,128)} %param.20) | copy-start | bytes 49156
  7.2 12.7 %copy-start.27 = (f32[512]{0:T(512)S(1)}, f32[512]{0:T(512)}, u32[]{:S(2)}) copy-start(f32[512]{0:T(512)} %param.18) | copy-start | bytes 6148
  7.2 13.6 %copy-start.11 = (s32[3,16384]{1,0:T(4,128)S(1)}, s32[3,16384]{1,0:T(4,128)}, u32[]{:S(2)}) copy-start(s32[3,16384]{1,0:T(4,128)} %param.22) | copy-start | bytes 589828
  7.2 98.8 %reduce-scatter.2.cloned.1.call-start = ((), (), s32[]{:S(2)}) async-start(), calls=%async_computation.1 | async-start | bytes 2162688 | tf_op jit(solution)/shard_map/reduce_scatter | solution.py:257
  12.3 345.8 %all-reduce.5.cloned.1.call-start = ((), (), s32[]{:S(2)}) async-start(), calls=%async_computation.2 | async-start | bytes 262144 | tf_op jit(solution)/shard_map/psum | solution.py:94
  14.6 391.4 %collective-permute-start.3 = (bf16[1,192,240]{2,1,0:T(8,128)(2,1)S(1)}, bf16[1,192,240]{2,1,0:T(8,128)(2,1)S(1)}, u32[]{:S(2)}, u32[]{:S(2)}) collective-permute-start(bf16[1,192,240]{2,1,0:T(8,128)(2,1)S(1)} %get-tuple-element.38), channel_id=1, source_target_pairs={{1,0},{2,1},{3,2},{4,3},{5,4},{6,5},{7,6},{0,7},{9,8},{10,9},{11,1... | collective-permute-start | bytes 276488 | tf_op jit(solution)/shard_map/ppermute | solution.py:25
  19.1 387.0 %collective-permute-start.2 = (bf16[1,192,240]{2,1,0:T(8,128)(2,1)S(1)}, bf16[1,192,240]{2,1,0:T(8,128)(2,1)S(1)}, u32[]{:S(2)}, u32[]{:S(2)}) collective-permute-start(bf16[1,192,240]{2,1,0:T(8,128)(2,1)S(1)} %get-tuple-element.37), channel_id=1, source_target_pairs={{0,1},{1,2},{2,3},{3,4},{4,5},{5,6},{6,7},{7,0},{8,9},{9,10},{10,1... | collective-permute-start | bytes 276488 | tf_op jit(solution)/shard_map/ppermute | solution.py:23
  19.3 425.8 %copy-start.22 = (f32[16]{0:T(128)}, f32[16]{0:T(128)S(1)}, u32[]{:S(2)}) copy-start(f32[16]{0:T(128)S(1)} %power_multiply_fusion) | copy-start | bytes 196
  401.6 4.4 copy-start.6
  402.3 3.8 copy-start.9
  403.5 30.0 %collective-permute-start.1 = (f32[3,1,192]{0,2,1:T(8,128)S(1)}, f32[3,1,192]{0,2,1:T(8,128)S(1)}, u32[]{:S(2)}, u32[]{:S(2)}) collective-permute-start(f32[3,1,192]{0,2,1:T(8,128)S(1)} %get-tuple-element.36), channel_id=1, source_target_pairs={{1,0},{2,1},{3,2},{4,3},{5,4},{6,5},{7,6},{0,7},{9,8},{10,9},{11,1... | collective-permute-start | bytes 6920 | tf_op jit(solution)/shard_map/ppermute | solution.py:25
  405.4 28.1 %collective-permute-start = (f32[3,1,192]{0,2,1:T(8,128)S(1)}, f32[3,1,192]{0,2,1:T(8,128)S(1)}, u32[]{:S(2)}, u32[]{:S(2)}) collective-permute-start(f32[3,1,192]{0,2,1:T(8,128)S(1)} %get-tuple-element.35), channel_id=1, source_target_pairs={{0,1},{1,2},{2,3},{3,4},{4,5},{5,6},{6,7},{7,0},{8,9},{9,10},{10,1... | collective-permute-start | bytes 6920 | tf_op jit(solution)/shard_map/ppermute | solution.py:23
  432.8 12.3 %copy-start.18 = (bf16[2,16,240]{2,1,0:T(8,128)(2,1)S(1)}, bf16[2,16,240]{2,1,0:T(8,128)(2,1)}, u32[]{:S(2)}) copy-start(bf16[2,16,240]{2,1,0:T(8,128)(2,1)} %param.23) | copy-start | bytes 46084
  444.4 3.7 copy-start.16
  444.4 3.9 copy-start.15
  444.4 3.9 copy-start.28
  448.0 1.6 copy-start.2
  448.0 8.2 %copy-start.23 = (f32[16]{0:T(128)S(1)}, f32[16]{0:T(128)}, u32[]{:S(2)}) copy-start(f32[16]{0:T(128)} %copy-done.22) | copy-start | bytes 196
  448.1 10.8 %copy-start.19 = (f32[512]{0:T(512)}, f32[512]{0:T(512)S(1)}, u32[]{:S(2)}) copy-start(f32[512]{0:T(512)S(1)} %multiply_reduce_fusion.6) | copy-start | bytes 6148
  448.4 1.2 copy-start.13
  452.0 7.8 %collective-permute-start.5 = (bf16[1,192,240]{1,2,0:T(8,128)(2,1)S(1)}, bf16[1,192,240]{1,2,0:T(8,128)(2,1)S(1)}, u32[]{:S(2)}, u32[]{:S(2)}) collective-permute-start(bf16[1,192,240]{1,2,0:T(8,128)(2,1)S(1)} %get-tuple-element.40), channel_id=1, source_target_pairs={{1,0},{2,1},{3,2},{4,3},{5,4},{6,5},{7,6},{0,7},{9,8},{10,9},{11,1... | collective-permute-start | bytes 276488 | tf_op jit(solution)/shard_map/ppermute | solution.py:25
  456.1 7.1 %collective-permute-start.4 = (bf16[1,192,240]{1,2,0:T(8,128)(2,1)S(1)}, bf16[1,192,240]{1,2,0:T(8,128)(2,1)S(1)}, u32[]{:S(2)}, u32[]{:S(2)}) collective-permute-start(bf16[1,192,240]{1,2,0:T(8,128)(2,1)S(1)} %get-tuple-element.39), channel_id=1, source_target_pairs={{0,1},{1,2},{2,3},{3,4},{4,5},{5,6},{6,7},{7,0},{8,9},{9,10},{10,1... | collective-permute-start | bytes 276488 | tf_op jit(solution)/shard_map/ppermute | solution.py:23
  487.0 4.4 copy-start.17
  491.4 3.7 copy-start.29
  500.9 0.8 copy-start.8
  534.7 3.7 copy-start.4
  534.8 0.9 copy-start.12
  536.4 12.2 %collective-permute-start.7 = (bf16[1,192,240]{2,1,0:T(8,128)(2,1)}, bf16[1,192,240]{2,1,0:T(8,128)(2,1)S(1)}, u32[]{:S(2)}, u32[]{:S(2)}) collective-permute-start(bf16[1,192,240]{2,1,0:T(8,128)(2,1)} %get-tuple-element.30), channel_id=1, source_target_pairs={{1,0},{2,1},{3,2},{4,3},{5,4},{6,5},{7,6},{0,7},{9,8},{10,9},{11,1... | collective-permute-start | bytes 276488 | tf_op jit(solution)/shard_map/ppermute | solution.py:25
  537.5 11.1 %collective-permute-start.6 = (bf16[1,192,240]{2,1,0:T(8,128)(2,1)}, bf16[1,192,240]{2,1,0:T(8,128)(2,1)}, u32[]{:S(2)}, u32[]{:S(2)}) collective-permute-start(bf16[1,192,240]{2,1,0:T(8,128)(2,1)} %get-tuple-element.29), channel_id=1, source_target_pairs={{0,1},{1,2},{2,3},{3,4},{4,5},{5,6},{6,7},{7,0},{8,9},{9,10},{10,1... | collective-permute-start | bytes 276488 | tf_op jit(solution)/shard_map/ppermute | solution.py:23
  538.4 5.3 copy-start.24
  543.7 3.1 copy-start.5
  543.7 13.4 %copy-start.3 = (f32[512,240]{0,1:T(8,128)S(1)}, f32[512,240]{0,1:T(8,128)}, u32[]{:S(2)}) copy-start(f32[512,240]{0,1:T(8,128)} %copy-done.2) | copy-start | bytes 1474564
  546.8 12.9 %copy-start.20 = (f32[512]{0:T(512)S(1)}, f32[512]{0:T(512)}, u32[]{:S(2)}) copy-start(f32[512]{0:T(512)} %copy-done.19) | copy-start | bytes 6148
  548.6 12.2 %copy-start.25 = (f32[16]{0:T(128)S(1)}, f32[16]{0:T(128)}, u32[]{:S(2)}) copy-start(f32[16]{0:T(128)} %copy-done.22) | copy-start | bytes 196
  566.8 2.2 copy-start.1
  569.0 59.0 %copy-start.7 = (f32[512,195]{1,0:T(8,128)S(1)}, f32[512,195]{1,0:T(8,128)}, u32[]{:S(2)}) copy-start(f32[512,195]{1,0:T(8,128)} %copy-done.6) | copy-start | bytes 1198084
  569.0 59.0 %copy-start.10 = (f32[1,512,6]{2,1,0:T(8,128)S(1)}, f32[1,512,6]{2,1,0:T(8,128)}, u32[]{:S(2)}) copy-start(f32[1,512,6]{2,1,0:T(8,128)} %copy-done.9) | copy-start | bytes 36868
  617.6 6.8 %collective-permute-start.8 = (f32[1,3,192]{1,2,0:T(8,128)S(1)}, f32[1,3,192]{1,2,0:T(8,128)S(1)}, u32[]{:S(2)}, u32[]{:S(2)}) collective-permute-start(f32[1,3,192]{1,2,0:T(8,128)S(1)} %get-tuple-element.28), channel_id=1, source_target_pairs={{0,1},{1,2},{2,3},{3,4},{4,5},{5,6},{6,7},{7,0},{8,9},{9,10},{10,1... | collective-permute-start | bytes 6920 | tf_op jit(solution)/shard_map/ppermute | solution.py:23
  619.1 7.2 %collective-permute-start.9 = (f32[1,3,192]{1,2,0:T(8,128)S(1)}, f32[1,3,192]{1,2,0:T(8,128)S(1)}, u32[]{:S(2)}, u32[]{:S(2)}) collective-permute-start(f32[1,3,192]{1,2,0:T(8,128)S(1)} %get-tuple-element.27), channel_id=1, source_target_pairs={{1,0},{2,1},{3,2},{4,3},{5,4},{6,5},{7,6},{0,7},{9,8},{10,9},{11,1... | collective-permute-start | bytes 6920 | tf_op jit(solution)/shard_map/ppermute | solution.py:25
Sparse Core Ops, SparseCore 0:
  12.4 93.5 reduce-scatter.1
  117.8 240.2 all-reduce.4
where the time goes:
time: 645 us; the launch traced here: 637 us
  waiting for transfers between devices  332 us (51%)
  other arithmetic  107 us (17%)
  local copies, waits for them, and re-layouts  88.1 us (14%)
  blocking collectives  41 us (6%)
  matrix products  35.9 us (6%)
  starting transfers between devices  17.5 us (3%)
  between operations  15 us (2%)
    psum x1, waiting for transfers between devices, long_range(): cosine_sum, sine_sum = lax.psum((cosine_part, sine_part), ('bead', 'dom'))  240 us
    reduce_scatter x1, waiting for transfers between devices, local(): lax.psum_scatter(jnp.einsum('bk,cba->ack', bead_rows, segment, precision=...  85 us
    gather x6, local copies, waits for them, and re-layouts, layer_apply(): message = jnp.sum(edge_weight * extended_rows[neighbour_table], 0)  53.4 us
    scatter-add x2, other arithmetic, layer_apply(): others = extended_coords[:, neighbour_table]  44.7 us
    all_gather x1, blocking collectives, local(): segment = lax.all_gather(packed, 'bead', axis=0, tiled=True)  41 us
    scatter-add x1, other arithmetic, layer_apply(): message = jnp.sum(edge_weight * extended_rows[neighbour_table], 0)  23.1 us
    ppermute x5, starting transfers between devices, extended(): lax.ppermute(head, axis, [((i + 1) % count, i) for i in range(count)])  14.3 us
  transfers between devices with their start and end apart: 12, of which 5 were waited for; matrix products, arithmetic and copies ran while one was open for 10% of the time, Pallas kernels for 0%

commit v1 on v0

--- a/solution.py
+++ b/solution.py
@@ -91,7 +91,7 @@
 
 def long_range(reciprocal, centre, charge, damping):
     cosine_part, sine_part = phase_sums(reciprocal, centre, charge)
-    cosine_sum, sine_sum = lax.psum((cosine_part, sine_part), ("bead", "dom"))
+    cosine_sum, sine_sum = lax.psum(lax.psum((cosine_part, sine_part), "bead"), "dom")
     return ewald_force(reciprocal, centre, charge, cosine_sum, sine_sum, damping)
 
 

time: 645 us -> 749 us (1.16)
  waiting for transfers between devices: 332 us -> 433 us
    psum x1 -> x2, waiting for transfers between devices: 240 us -> 341 us  [the longest x1 257 us: long_range(): lax.psum((cosine_part, sine_part), 'bead')]
  transfers between devices with their start and end apart: 12 -> 13, of which waited for: 5 -> 6; matrix products, arithmetic and copies ran while one was open for 10% -> 8% of each run, Pallas kernels for 0% -> 0%
where the time goes in v1:
time: 749 us; the launch traced here: 738 us
  waiting for transfers between devices  433 us (58%)
  other arithmetic  107 us (14%)
  local copies, waits for them, and re-layouts  88.4 us (12%)
  blocking collectives  40.9 us (5%)
  matrix products  36 us (5%)
  starting transfers between devices  17.9 us (2%)
  between operations  14.7 us (2%)
    psum x1, waiting for transfers between devices, long_range(): lax.psum((cosine_part, sine_part), 'bead')  257 us
    reduce_scatter x1, waiting for transfers between devices, local(): lax.psum_scatter(jnp.einsum('bk,cba->ack', bead_rows, segment, precision=...  85.2 us
    psum x1, waiting for transfers between devices, long_range(): lax.psum(lax.psum((cosine_part, sine_part), 'bead'), 'dom')  83.5 us
    gather x6, local copies, waits for them, and re-layouts, layer_apply(): message = jnp.sum(edge_weight * extended_rows[neighbour_table], 0)  53.6 us
    scatter-add x2, other arithmetic, layer_apply(): others = extended_coords[:, neighbour_table]  44.7 us
    all_gather x1, blocking collectives, local(): segment = lax.all_gather(packed, 'bead', axis=0, tiled=True)  40.9 us
    scatter-add x1, other arithmetic, layer_apply(): message = jnp.sum(edge_weight * extended_rows[neighbour_table], 0)  23.1 us
  transfers between devices with their start and end apart: 13, of which 6 were waited for; matrix products, arithmetic and copies ran while one was open for 8% of the time, Pallas kernels for 0%

profile of v1, /device:TPU:2, one launch (start us, length us, event | category | flops | bytes accessed | tf_op | source)
XLA Modules:
  0.0 737.9 jit_solution(12056500386306194404)
XLA Ops:
  10.3 2.0 multiply_bitcast_fusion
  12.5 2.1 gather_fusion.2
  14.6 4.4 collective-permute-start.3
  20.8 85.2 %reduce-scatter.2.cloned.1.call-done = f32[16,6,32]{2,1,0:T(8,128)} async-done(((f32[512,6,32]{2,1,0:T(8,128)}), f32[16,6,32]{2,1,0:T(8,128)}) %reduce-scatter.2.cloned.1.call-update) | async-done | bytes 12304 | tf_op jit(solution)/shard_map/reduce_scatter | solution.py:257
  107.0 8.0 %fusion.207 = (f32[16384,16]{0,1:T(8,128)S(1)}, f32[16384,16]{0,1:T(8,128)S(1)}) fusion(f32[3,16]{1,0:T(4,128)S(1)} %fusion.160, s32[3,16384]{1,0:T(4,128)S(1)} %copy-done.11), kind=kOutput, calls=%fused_computation.258 | convolution fusion | flops 9535488 | bytes 2293952 | tf_op jit(solution)/shard_map/dot_general | solution.py:77
  115.0 1.3 fusion.186
  116.3 1.3 fusion.188
  117.9 257.2 %all-reduce.7.cloned.1.call-done = (f32[16384]{0:T(1024)}, f32[16384]{0:T(1024)}) async-done(((f32[16384]{0:T(1024)}, f32[16384]{0:T(1024)}), (f32[16384]{0:T(1024)}, f32[16384]{0:T(1024)})) %all-reduce.7.cloned.1.call-update) | async-done | bytes 131088 | tf_op jit(solution)/shard_map/psum | solution.py:94
  375.2 83.5 %all-reduce.9.cloned.1.call-done = (f32[16384]{0:T(1024)}, f32[16384]{0:T(1024)}) async-done(((f32[16384]{0:T(1024)}, f32[16384]{0:T(1024)}), (f32[16384]{0:T(1024)}, f32[16384]{0:T(1024)})) %all-reduce.9.cloned.1.call-update) | async-done | bytes 131088 | tf_op jit(solution)/shard_map/psum | solution.py:94
  459.6 1.4 convolution_multiply_fusion
  461.2 40.9 %all_gather.3 = f32[512,195]{1,0:T(8,128)S(1)} all-gather(f32[16,195]{1,0:T(8,128)S(1)} %pad_maximum_fusion.5), channel_id=1, replica_groups=mesh['bead'=32,'dom'=8] {'bead'}, dimensions={0}, use_global_device_ids=true | all-gather | bytes 411840 | tf_op jit(solution)/shard_map/all_gather | solution.py:268
  504.0 2.3 collective-permute-start.1
  506.9 16.2 %gather_fusion.3 = f32[4096,240]{1,0:T(8,128)} fusion(f32[896,240]{1,0:T(8,128)S(1)} %fusion.95, s32[4096]{0:T(1024)S(1)} %broadcast_clamp_fusion), kind=kCustom, calls=%fused_computation.3 | custom fusion | bytes 7880704 | tf_op jit(solution)/shard_map/vmap()/gather | solution.py:124
  523.0 5.3 copy.144
  528.3 5.3 copy.134
  534.4 10.8 %gather_fusion.1 = f32[4096,3]{1,0:T(8,128)S(1)} fusion(f32[3,896]{0,1:T(8,128)S(1)} %get-tuple-element.34, s32[4096]{0:T(1024)S(1)} %broadcast_clamp_fusion), kind=kCustom, calls=%fused_computation.1 | custom fusion | bytes 114688 | tf_op jit(solution)/shard_map/jvp(vmap())/gather | solution.py:119
  545.9 2.9 multiply_reduce_fusion.1
  550.5 2.1 gather_fusion.4
  552.8 4.2 collective-permute-start.5
  557.2 2.6 fusion.124
  560.8 3.4 collective-permute-done.4
  565.2 1.5 copy.137
  566.6 16.2 %gather_fusion.5 = f32[4096,240]{1,0:T(8,128)} fusion(f32[896,240]{1,0:T(8,128)S(1)} %copy.137, s32[4096]{0:T(1024)S(1)} %broadcast_clamp_fusion), kind=kCustom, calls=%fused_computation.5 | custom fusion | bytes 7880704 | tf_op jit(solution)/shard_map/vmap()/gather | solution.py:124
  582.8 5.3 copy.139
  588.1 4.4 multiply_reduce_fusion
  593.6 2.6 fusion.13
  596.2 2.1 convolution_convert_fusion.4
  598.3 2.5 multiply_reduce_fusion.4
  602.8 4.7 broadcast_multiply_fusion
  607.5 5.2 copy.154
  612.8 23.1 %scatter_custom_fusion.1 = f32[896,240]{1,0:T(8,128)S(1)} fusion(s32[4096]{0:T(1024)S(1)} %bitcast.302, f32[4096,240]{1,0:T(8,128)} %bitcast.291, f32[]{:T(128)} %constant.51.clone.1), kind=kCustom, calls=%fused_computation.103 | custom fusion | flops 983040 | bytes 860672 | tf_op jit(solution)/shard_map/transpose(jvp(vmap()))/scatter-add | solution.py:124
  637.5 1.2 collective-permute-start.7
  639.5 5.3 copy.140
  644.9 3.1 fusion.59
  649.8 3.9 scatter_custom_fusion.2
  653.7 3.5 scatter_custom_fusion.3
  657.1 1.2 copy.143
  658.3 2.5 multiply_reduce_fusion.3
  662.0 2.8 fusion.38
  664.9 3.2 add_multiply_fusion
  668.1 1.9 reduce_sum.128
  673.0 22.8 %scatter_fusion = f32[3,896]{0,1:T(8,128)S(1)} fusion(f32[3,896]{0,1:T(8,128)S(1)} %pad_bitcast_fusion.1, s32[4096]{0:T(1024)S(1)} %bitcast.303, f32[4096,3]{1,0:T(8,128)} %bitcast.288), kind=kCustom, calls=%fused_computation.6 | custom fusion | flops 12288 | bytes 163840 | tf_op jit(solution)/shard_map/transpose(jvp(vmap()))/scatter-add | solution.py:119
  695.8 21.9 %scatter_fusion.1 = f32[3,896]{0,1:T(8,128)} fusion(f32[3,896]{0,1:T(8,128)} %pad_bitcast_fusion, s32[4096]{0:T(1024)S(1)} %bitcast.304, f32[4096,3]{1,0:T(8,128)S(1)} %bitcast.287), kind=kCustom, calls=%fused_computation.10 | custom fusion | flops 12288 | bytes 163840 | tf_op jit(solution)/shard_map/transpose(jvp(vmap()))/scatter-add | solution.py:119
  718.8 1.5 collective-permute-start.8
  720.3 2.7 collective-permute-start.9
  723.1 2.6 collective-permute-done.8
  725.6 1.8 scatter_custom_fusion.5
  727.5 1.9 scatter_custom_fusion.6
  (151 shorter events, 29.6 us)
Async XLA Ops:
  7.2 586.5 %copy-start = (bf16[240,240]{1,0:T(8,128)(2,1)S(1)}, bf16[240,240]{1,0:T(8,128)(2,1)}, u32[]{:S(2)}) copy-start(bf16[240,240]{1,0:T(8,128)(2,1)} %param.26) | copy-start | bytes 345604
  7.2 5.1 copy-start.14
  7.2 5.3 copy-start.25
  7.2 12.6 %copy-start.21 = (s32[8,512]{1,0:T(8,128)S(1)}, s32[8,512]{1,0:T(8,128)}, u32[]{:S(2)}) copy-start(s32[8,512]{1,0:T(8,128)} %param.20) | copy-start | bytes 49156
  7.2 12.6 %copy-start.26 = (f32[512]{0:T(512)S(1)}, f32[512]{0:T(512)}, u32[]{:S(2)}) copy-start(f32[512]{0:T(512)} %param.18) | copy-start | bytes 6148
  7.2 98.8 %reduce-scatter.2.cloned.1.call-start = ((), (), s32[]{:S(2)}) async-start(), calls=%async_computation.1 | async-start | bytes 2162688 | tf_op jit(solution)/shard_map/reduce_scatter | solution.py:257
  7.3 99.7 %copy-start.11 = (s32[3,16384]{1,0:T(4,128)S(1)}, s32[3,16384]{1,0:T(4,128)}, u32[]{:S(2)}) copy-start(s32[3,16384]{1,0:T(4,128)} %param.22) | copy-start | bytes 589828
  12.3 362.8 %all-reduce.7.cloned.1.call-start = ((), (), s32[]{:S(2)}) async-start(), calls=%async_computation.2 | async-start | bytes 262144 | tf_op jit(solution)/shard_map/psum | solution.py:94
  14.6 492.2 %collective-permute-start.3 = (bf16[1,192,240]{2,1,0:T(8,128)(2,1)S(1)}, bf16[1,192,240]{2,1,0:T(8,128)(2,1)S(1)}, u32[]{:S(2)}, u32[]{:S(2)}) collective-permute-start(bf16[1,192,240]{2,1,0:T(8,128)(2,1)S(1)} %get-tuple-element.40), channel_id=1, source_target_pairs={{1,0},{2,1},{3,2},{4,3},{5,4},{6,5},{7,6},{0,7},{9,8},{10,9},{11,1... | collective-permute-start | bytes 276488 | tf_op jit(solution)/shard_map/ppermute | solution.py:25
  19.0 487.7 %collective-permute-start.2 = (bf16[1,192,240]{2,1,0:T(8,128)(2,1)S(1)}, bf16[1,192,240]{2,1,0:T(8,128)(2,1)S(1)}, u32[]{:S(2)}, u32[]{:S(2)}) collective-permute-start(bf16[1,192,240]{2,1,0:T(8,128)(2,1)S(1)} %get-tuple-element.39), channel_id=1, source_target_pairs={{0,1},{1,2},{2,3},{3,4},{4,5},{5,6},{6,7},{7,0},{8,9},{9,10},{10,1... | collective-permute-start | bytes 276488 | tf_op jit(solution)/shard_map/ppermute | solution.py:23
  117.6 341.1 %all-reduce.9.cloned.1.call-start = ((), (), s32[]{:S(2)}) async-start(), calls=%async_computation.3 | async-start | bytes 262144 | tf_op jit(solution)/shard_map/psum | solution.py:94
  375.1 182.1 %copy-start.22 = (f32[16]{0:T(128)}, f32[16]{0:T(128)S(1)}, u32[]{:S(2)}) copy-start(f32[16]{0:T(128)S(1)} %power_multiply_fusion) | copy-start | bytes 196
  502.1 4.7 copy-start.6
  502.8 4.0 copy-start.9
  504.0 30.4 %collective-permute-start.1 = (f32[3,1,192]{0,2,1:T(8,128)S(1)}, f32[3,1,192]{0,2,1:T(8,128)S(1)}, u32[]{:S(2)}, u32[]{:S(2)}) collective-permute-start(f32[3,1,192]{0,2,1:T(8,128)S(1)} %get-tuple-element.38), channel_id=1, source_target_pairs={{1,0},{2,1},{3,2},{4,3},{5,4},{6,5},{7,6},{0,7},{9,8},{10,9},{11,1... | collective-permute-start | bytes 6920 | tf_op jit(solution)/shard_map/ppermute | solution.py:25
  506.3 28.1 %collective-permute-start = (f32[3,1,192]{0,2,1:T(8,128)S(1)}, f32[3,1,192]{0,2,1:T(8,128)S(1)}, u32[]{:S(2)}, u32[]{:S(2)}) collective-permute-start(f32[3,1,192]{0,2,1:T(8,128)S(1)} %get-tuple-element.37), channel_id=1, source_target_pairs={{0,1},{1,2},{2,3},{3,4},{4,5},{5,6},{6,7},{7,0},{8,9},{9,10},{10,1... | collective-permute-start | bytes 6920 | tf_op jit(solution)/shard_map/ppermute | solution.py:23
  533.6 12.3 %copy-start.18 = (bf16[2,16,240]{2,1,0:T(8,128)(2,1)S(1)}, bf16[2,16,240]{2,1,0:T(8,128)(2,1)}, u32[]{:S(2)}) copy-start(bf16[2,16,240]{2,1,0:T(8,128)(2,1)} %param.23) | copy-start | bytes 46084
  545.2 3.7 copy-start.16
  545.3 3.9 copy-start.15
  545.3 3.9 copy-start.27
  548.8 1.6 copy-start.2
  548.9 10.9 %copy-start.19 = (f32[512]{0:T(512)}, f32[512]{0:T(512)S(1)}, u32[]{:S(2)}) copy-start(f32[512]{0:T(512)S(1)} %multiply_reduce_fusion.6) | copy-start | bytes 6148
  549.2 1.2 copy-start.13
  552.8 7.9 %collective-permute-start.5 = (bf16[1,192,240]{1,2,0:T(8,128)(2,1)S(1)}, bf16[1,192,240]{1,2,0:T(8,128)(2,1)S(1)}, u32[]{:S(2)}, u32[]{:S(2)}) collective-permute-start(bf16[1,192,240]{1,2,0:T(8,128)(2,1)S(1)} %get-tuple-element.42), channel_id=1, source_target_pairs={{1,0},{2,1},{3,2},{4,3},{5,4},{6,5},{7,6},{0,7},{9,8},{10,9},{11,1... | collective-permute-start | bytes 276488 | tf_op jit(solution)/shard_map/ppermute | solution.py:25
  557.0 7.1 collective-permute-start.4
  588.1 4.4 copy-start.17
  592.5 3.8 copy-start.28
  602.0 0.8 copy-start.8
  635.8 3.7 copy-start.4
  635.9 0.9 copy-start.12
  637.5 12.2 %collective-permute-start.7 = (bf16[1,192,240]{2,1,0:T(8,128)(2,1)}, bf16[1,192,240]{2,1,0:T(8,128)(2,1)S(1)}, u32[]{:S(2)}, u32[]{:S(2)}) collective-permute-start(bf16[1,192,240]{2,1,0:T(8,128)(2,1)} %get-tuple-element.32), channel_id=1, source_target_pairs={{1,0},{2,1},{3,2},{4,3},{5,4},{6,5},{7,6},{0,7},{9,8},{10,9},{11,1... | collective-permute-start | bytes 276488 | tf_op jit(solution)/shard_map/ppermute | solution.py:25
  638.7 11.1 %collective-permute-start.6 = (bf16[1,192,240]{2,1,0:T(8,128)(2,1)}, bf16[1,192,240]{2,1,0:T(8,128)(2,1)}, u32[]{:S(2)}, u32[]{:S(2)}) collective-permute-start(bf16[1,192,240]{2,1,0:T(8,128)(2,1)} %get-tuple-element.31), channel_id=1, source_target_pairs={{0,1},{1,2},{2,3},{3,4},{4,5},{5,6},{6,7},{7,0},{8,9},{9,10},{10,1... | collective-permute-start | bytes 276488 | tf_op jit(solution)/shard_map/ppermute | solution.py:23
  639.5 5.3 copy-start.23
  644.9 3.1 copy-start.5
  644.9 13.4 %copy-start.3 = (f32[512,240]{0,1:T(8,128)S(1)}, f32[512,240]{0,1:T(8,128)}, u32[]{:S(2)}) copy-start(f32[512,240]{0,1:T(8,128)} %copy-done.2) | copy-start | bytes 1474564
  648.0 12.9 %copy-start.20 = (f32[512]{0:T(512)S(1)}, f32[512]{0:T(512)}, u32[]{:S(2)}) copy-start(f32[512]{0:T(512)} %copy-done.19) | copy-start | bytes 6148
  649.8 12.3 %copy-start.24 = (f32[16]{0:T(128)S(1)}, f32[16]{0:T(128)}, u32[]{:S(2)}) copy-start(f32[16]{0:T(128)} %copy-done.22) | copy-start | bytes 196
  668.1 2.2 copy-start.1
  670.3 59.0 %copy-start.7 = (f32[512,195]{1,0:T(8,128)S(1)}, f32[512,195]{1,0:T(8,128)}, u32[]{:S(2)}) copy-start(f32[512,195]{1,0:T(8,128)} %copy-done.6) | copy-start | bytes 1198084
  670.3 59.1 %copy-start.10 = (f32[1,512,6]{2,1,0:T(8,128)S(1)}, f32[1,512,6]{2,1,0:T(8,128)}, u32[]{:S(2)}) copy-start(f32[1,512,6]{2,1,0:T(8,128)} %copy-done.9) | copy-start | bytes 36868
  718.8 6.8 collective-permute-start.8
  720.3 7.2 collective-permute-start.9
Sparse Core Ops, SparseCore 0:
  12.4 93.5 reduce-scatter.1
  117.8 257.2 all-reduce.6
  377.9 80.7 all-reduce.8
